TPU v7x, 256 devices: a whole 4x4x8 slice. The times are simulated.
256 devices in a mesh: grp: 32 (over y, x, core), bal: 8 (over z).
Axes of the slice: x: 4, y: 4, z: 8, core: 2. Of those that a mesh axis runs over, the one named last changes fastest.
Arguments:
- grad_out: float32 [32768, 256], P(('grp', 'bal')), may hold values from -6 to 6
- deriv_mask: int32 [32768, 256], P(('grp', 'bal')), may hold values 0 or 1
- weight: float32 [256, 256], replicated, may hold values from -0.375 to 0.375
- zcache: float32 [32768, 256], P(('grp', 'bal')), may hold values from -0.03125 to 0.03125
- tile_values: float32 [8192, 128, 128], P(('grp', 'bal')), may hold values from -0.09375 to 0.09375
- tile_source: int32 [8192], P(('grp', 'bal')), may hold values from 0 to 7
- tile_slot: int32 [8192], P(('grp', 'bal')), may hold values from 0 to 63, as said below
- recv_target: int32 [16384], P(('grp', 'bal')), may hold values from -1 to 7, as said below
Outputs:
- weight_grad: float32 [256, 256], replicated
- fixed_grad: float32 [32768, 256], P(('grp', 'bal'))
Inputs may be any that keep to these rules, and one draw needn't show every extreme that they name: Each device's tile_slot values are distinct, so at most 2 tiles go from one device to one row group; every device fills all 2 slots toward some row group. recv_target is -1 exactly at the slots that no tile_slot of the sending device names, and a block index within the row group elsewhere.
All inputs are finite; a program needn't handle non-finite values. No bound on the sum of `deriv_mask` on one device may be relied on, other than what follows from the above.
Results may differ from a plain program's by a relative error of at most 0.0001.
Values sent between devices are 32-bit elements; how exact they have to be, the bound alone decides.
No kernel may reach another device: no remote copies, remote signals or barrier semaphores. Data moves between devices by JAX's collectives and lax.ppermute only.
A program may use at most 128 MiB of HBM per device.

v0:
```python
import jax
import jax.numpy as jnp
from jax import lax
from jax.sharding import PartitionSpec as P

STEPS = 3


def per_device(
    grad_out, deriv_mask, weight, zcache, tile_values, tile_source, tile_slot, recv_target
):
    rows, width = grad_out.shape
    blk = tile_values.shape[1]
    n_bal = lax.axis_size("bal")
    per_group = rows // blk * n_bal
    slots = recv_target.shape[0]
    highest = lax.Precision.HIGHEST
    selector = (recv_target[:, None] == jnp.arange(per_group, dtype=jnp.int32)[None, :]).astype(
        jnp.float32
    )
    mask_float = deriv_mask.astype(jnp.float32)
    fixed_grad = grad_out
    for step in range(STEPS):
        group_rows = lax.all_gather(fixed_grad, "bal", axis=0, tiled=True)
        blocks = group_rows.reshape(per_group, blk, width)
        partial_value = jnp.einsum(
            "tij,tjf->tif", tile_values, blocks[tile_source], precision=highest
        )
        outgoing = jnp.zeros((slots, blk, width), jnp.float32).at[tile_slot].set(partial_value)
        incoming = lax.all_to_all(outgoing, "grp", split_axis=0, concat_axis=0, tiled=True)
        sums = jnp.einsum("st,sif->tif", selector, incoming, precision=highest)
        owned = lax.psum_scatter(sums, "bal", scatter_dimension=0, tiled=True).reshape(rows, width)
        product = jnp.dot(owned, weight, precision=highest, preferred_element_type=jnp.float32)
        fixed_grad = mask_float * product + grad_out
    local_term = jnp.dot(
        fixed_grad.T, zcache, precision=highest, preferred_element_type=jnp.float32
    )
    weight_grad = lax.psum(local_term, ("grp", "bal"))
    return (weight_grad, fixed_grad)


def solution(mesh):
    in_specs = (
        P(("grp", "bal"), None),
        P(("grp", "bal"), None),
        P(),
        P(("grp", "bal"), None),
        P(("grp", "bal"), None, None),
        P(("grp", "bal")),
        P(("grp", "bal")),
        P(("grp", "bal")),
    )
    out_specs = (P(), P(("grp", "bal"), None))
    return jax.shard_map(
        per_device, mesh=mesh, in_specs=in_specs, out_specs=out_specs, check_vma=False
    )
```

profile of v0, /device:TPU:1, one launch (start us, length us, event | category | flops | bytes accessed | tf_op | source)
XLA Modules:
  0.0 909.9 jit_solution(842472673003495016)
XLA Ops:
  9.3 38.0 %all-gather.4.cloned.1.call-done = f32[1024,256]{1,0:T(8,128)} async-done(((f32[128,256]{1,0:T(8,128)}), f32[1024,256]{1,0:T(8,128)}) %all-gather.4.cloned.1.call-update) | async-done | bytes 1048592 | tf_op jit(solution)/shard_map/all_gather | solution.py:24
  47.3 4.0 gather_fusion
  51.3 8.1 convolution_bitcast_fusion.2
  59.4 4.3 broadcast.13.clone.1
  63.6 8.4 scatter_fusion
  72.0 108.9 %all_to_all.15 = f32[64,128,256]{2,1,0:T(8,128)S(1)} all-to-all(f32[64,128,256]{2,1,0:T(8,128)} %scatter_fusion), channel_id=1, replica_groups=mesh['grp'=32,'bal'=8] {'grp'}, dimensions={0} | all-to-all | bytes 16777216 | tf_op jit(solution)/shard_map/all_to_all | solution.py:30
  180.9 7.5 fusion.4
  189.8 30.1 %reduce-scatter.4.cloned.1.call-done = f32[1,128,256]{2,1,0:T(8,128)} async-done(((f32[8,128,256]{2,1,0:T(8,128)}), f32[1,128,256]{2,1,0:T(8,128)}) %reduce-scatter.4.cloned.1.call-update) | async-done | bytes 131088 | tf_op jit(solution)/shard_map/reduce_scatter | solution.py:32
  222.3 36.8 %all-gather.6.cloned.1.call-done = f32[1024,256]{1,0:T(8,128)} async-done(((f32[128,256]{1,0:T(8,128)}), f32[1024,256]{1,0:T(8,128)}) %all-gather.6.cloned.1.call-update) | async-done | bytes 1048592 | tf_op jit(solution)/shard_map/all_gather | solution.py:24
  259.1 4.0 gather_fusion.1
  263.1 8.1 convolution_bitcast_fusion.1
  271.2 4.3 broadcast.13.clone
  275.5 8.4 scatter_fusion.1
  283.8 108.7 %all_to_all.16 = f32[64,128,256]{2,1,0:T(8,128)S(1)} all-to-all(f32[64,128,256]{2,1,0:T(8,128)} %scatter_fusion.1), channel_id=1, replica_groups=mesh['grp'=32,'bal'=8] {'grp'}, dimensions={0} | all-to-all | bytes 16777216 | tf_op jit(solution)/shard_map/all_to_all | solution.py:30
  392.5 7.5 fusion.2
  401.4 29.6 %reduce-scatter.6.cloned.1.call-done = f32[1,128,256]{2,1,0:T(8,128)} async-done(((f32[8,128,256]{2,1,0:T(8,128)}), f32[1,128,256]{2,1,0:T(8,128)}) %reduce-scatter.6.cloned.1.call-update) | async-done | bytes 131088 | tf_op jit(solution)/shard_map/reduce_scatter | solution.py:32
  433.1 37.4 %all-gather.8.cloned.1.call-done = f32[1024,256]{1,0:T(8,128)} async-done(((f32[128,256]{1,0:T(8,128)}), f32[1024,256]{1,0:T(8,128)}) %all-gather.8.cloned.1.call-update) | async-done | bytes 1048592 | tf_op jit(solution)/shard_map/all_gather | solution.py:24
  474.5 8.1 convolution_bitcast_fusion
  482.7 4.3 broadcast.13
  486.9 8.4 scatter_fusion.2
  495.3 108.8 %all_to_all.17 = f32[64,128,256]{2,1,0:T(8,128)S(1)} all-to-all(f32[64,128,256]{2,1,0:T(8,128)} %scatter_fusion.2), channel_id=1, replica_groups=mesh['grp'=32,'bal'=8] {'grp'}, dimensions={0} | all-to-all | bytes 16777216 | tf_op jit(solution)/shard_map/all_to_all | solution.py:30
  604.0 7.5 fusion
  612.9 30.1 %reduce-scatter.8.cloned.1.call-done = f32[1,128,256]{2,1,0:T(8,128)} async-done(((f32[8,128,256]{2,1,0:T(8,128)}), f32[1,128,256]{2,1,0:T(8,128)}) %reduce-scatter.8.cloned.1.call-update) | async-done | bytes 131088 | tf_op jit(solution)/shard_map/reduce_scatter | solution.py:32
  645.3 255.8 %all-reduce.2.cloned.1.call-done = f32[256,256]{1,0:T(8,128)} async-done(((f32[256,256]{1,0:T(8,128)}), f32[256,256]{1,0:T(8,128)}) %all-reduce.2.cloned.1.call-update) | async-done | bytes 262160 | tf_op jit(solution)/shard_map/psum | solution.py:38
  (40 shorter events, 18.7 us)
Async XLA Ops:
  7.2 44.1 %copy-start = (f32[32,128,128]{2,1,0:T(8,128)S(1)}, f32[32,128,128]{2,1,0:T(8,128)}, u32[]{:S(2)}) copy-start(f32[32,128,128]{2,1,0:T(8,128)} %param.12) | copy-start | bytes 6291460
  7.2 40.1 %all-gather.4.cloned.1.call-start = ((), (), s32[]{:S(2)}) async-start(), calls=%async_computation.6 | async-start | bytes 1179648 | tf_op jit(solution)/shard_map/all_gather | solution.py:24
  7.9 212.0 %reduce-scatter.4.cloned.1.call-start = ((), (), s32[]{:S(2)}) async-start(), calls=%async_computation.7 | async-start | bytes 1179648 | tf_op jit(solution)/shard_map/reduce_scatter | solution.py:32
  72.0 108.9 %copy-start.6 = (s32[64]{0:T(128)S(1)}, s32[64]{0:T(128)}, u32[]{:S(2)}) copy-start(s32[64]{0:T(128)} %param.15) | copy-start | bytes 772
  180.9 38.9 %copy-start.1 = (f32[256,256]{1,0:T(8,128)S(1)}, f32[256,256]{1,0:T(8,128)}, u32[]{:S(2)}) copy-start(f32[256,256]{1,0:T(8,128)} %param.10) | copy-start | bytes 786436
  180.9 38.9 %copy-start.2 = (f32[128,256]{1,0:T(8,128)S(1)}, f32[128,256]{1,0:T(8,128)}, u32[]{:S(2)}) copy-start(f32[128,256]{1,0:T(8,128)} %param.8) | copy-start | bytes 393220
  180.9 38.9 %copy-start.3 = (s32[128,256]{1,0:T(8,128)S(1)}, s32[128,256]{1,0:T(8,128)}, u32[]{:S(2)}) copy-start(s32[128,256]{1,0:T(8,128)} %param.9) | copy-start | bytes 393220
  189.8 69.4 %all-gather.6.cloned.1.call-start = ((), (), s32[]{:S(2)}) async-start(), calls=%async_computation.8 | async-start | bytes 1179648 | tf_op jit(solution)/shard_map/all_gather | solution.py:24
  221.7 209.3 %reduce-scatter.6.cloned.1.call-start = ((), (), s32[]{:S(2)}) async-start(), calls=%async_computation.9 | async-start | bytes 1179648 | tf_op jit(solution)/shard_map/reduce_scatter | solution.py:32
  401.3 69.2 %all-gather.8.cloned.1.call-start = ((), (), s32[]{:S(2)}) async-start(), calls=%async_computation.10 | async-start | bytes 1179648 | tf_op jit(solution)/shard_map/all_gather | solution.py:24
  432.9 210.1 %reduce-scatter.8.cloned.1.call-start = ((), (), s32[]{:S(2)}) async-start(), calls=%async_computation.11 | async-start | bytes 1179648 | tf_op jit(solution)/shard_map/reduce_scatter | solution.py:32
  604.0 40.1 %copy-start.5 = (f32[128,256]{1,0:T(8,128)S(1)}, f32[128,256]{1,0:T(8,128)}, u32[]{:S(2)}) copy-start(f32[128,256]{1,0:T(8,128)} %param.11) | copy-start | bytes 393220
  612.8 288.3 %all-reduce.2.cloned.1.call-start = ((), (), s32[]{:S(2)}) async-start(), calls=%async_computation.12 | async-start | bytes 524288 | tf_op jit(solution)/shard_map/psum | solution.py:38
  644.2 258.7 %copy-start.4 = (f32[128,256]{1,0:T(8,128)}, f32[128,256]{1,0:T(8,128)S(1)}, u32[]{:S(2)}) copy-start(f32[128,256]{1,0:T(8,128)S(1)} %fusion.6) | copy-start | bytes 393220
Sparse Core Ops, SparseCore 0:
  9.8 37.4 all-gather.3
  189.9 29.9 reduce-scatter.3
  222.2 36.8 all-gather.5
  401.5 29.5 reduce-scatter.5
  433.2 37.2 all-gather.7
  613.0 29.9 reduce-scatter.7
  649.0 252.1 all-reduce.1
where the time goes:
time: 916 us; the launch traced here: 910 us
  waiting for transfers between devices  459 us (50%)
  blocking collectives  326 us (36%)
  local copies, waits for them, and re-layouts  55.4 us (6%)
  matrix products  52.9 us (6%)
  between operations  14.4 us (2%)
    all_to_all x3, blocking collectives, per_device(): lax.all_to_all(outgoing, 'grp', split_axis=0, concat_axis=0, tiled=True)  326 us
    psum x1, waiting for transfers between devices, per_device(): weight_grad = lax.psum(local_term, ('grp', 'bal'))  256 us
    all_gather x3, waiting for transfers between devices, per_device(): group_rows = lax.all_gather(fixed_grad, 'bal', axis=0, tiled=True)  112 us
    reduce_scatter x3, waiting for transfers between devices, per_device(): lax.psum_scatter(sums, 'bal', scatter_dimension=0, tiled=True)  89.7 us
    scatter x3, local copies, waits for them, and re-layouts, per_device(): jnp.zeros((slots, blk, width), jnp.float32).at[tile_slot].set(partial_value)  25.1 us
    dot_general x3, matrix products, per_device(): jnp.einsum('tij,tjf->tif', tile_values, blocks[tile_source], precision=hi...  24.4 us
    dot_general x3, matrix products, per_device(): sums = jnp.einsum('st,sif->tif', selector, incoming, precision=highest)  22.5 us
  transfers between devices with their start and end apart: 7, of which 7 were waited for; matrix products, arithmetic and copies ran while one was open for 0% of the time, Pallas kernels for 0%

commit v1 on v0

v1 whole, which is shorter than its diff:
```python
import functools

import jax
import jax.numpy as jnp
from jax import lax
from jax.experimental import pallas as pl
from jax.experimental.pallas import tpu as pltpu
from jax.sharding import Mesh
from jax.sharding import PartitionSpec as P

STEPS = 3
BLK = 128
BUFS = 8
PLANE = ("y", "x")
GRP = ("y", "x", "core")
ALL = ("y", "x", "core", "bal")
HIGHEST = lax.Precision.HIGHEST


def split(value):
    high = value.astype(jnp.bfloat16)
    low = (value - high.astype(jnp.float32)).astype(jnp.bfloat16)
    return high, low


def products_kernel(count, place, source, target, *refs):
    n_blocks = len(refs) - 6
    blocks = refs[:n_blocks]
    tiles, keep, send, rhs, held, sems = refs[n_blocks:]
    chips = keep.shape[0] // BLK
    total = count[0]

    def copy(k, slot):
        return pltpu.make_async_copy(tiles.at[place[k]], held.at[slot], sems.at[slot])

    for slot in range(BUFS):

        @pl.when(slot < total)
        def _(slot=slot):
            copy(slot, slot).start()

    for i, block in enumerate(blocks):
        high, low = split(block[...])
        rhs[i, 0:BLK] = high
        rhs[i, BLK : 2 * BLK] = high
        rhs[i, 2 * BLK : 3 * BLK] = low
    keep[...] = jnp.zeros_like(keep)
    send[...] = jnp.zeros_like(send)

    def body(k, carry):
        slot = lax.rem(k, BUFS)
        copy(k, slot).wait()
        high, low = split(held[slot])
        lhs = jnp.concatenate([high, low, high], axis=1)
        product = jnp.dot(lhs, rhs[source[k]], preferred_element_type=jnp.float32)
        where = target[k]
        rows = pl.ds(pl.multiple_of(lax.rem(where, chips) * BLK, BLK), BLK)

        @pl.when(where < chips)
        def _():
            keep[rows] += product

        @pl.when(where >= chips)
        def _():
            send[rows] += product

        @pl.when(k + BUFS < total)
        def _():
            copy(k + BUFS, slot).start()

        return carry

    lax.fori_loop(0, total, body, 0)


def products(count, place, source, target, blocks, tiles, chips):
    width = blocks[0].shape[1]
    smem = pl.BlockSpec(memory_space=pltpu.SMEM)
    vmem = pl.BlockSpec(memory_space=pltpu.VMEM)
    out = jax.ShapeDtypeStruct((chips * BLK, width), jnp.float32)
    return pl.pallas_call(
        products_kernel,
        out_shape=(out, out),
        in_specs=[smem] * 4 + [vmem] * len(blocks) + [pl.BlockSpec(memory_space=pl.ANY)],
        out_specs=(vmem, vmem),
        scratch_shapes=[
            pltpu.VMEM((len(blocks), 3 * BLK, width), jnp.bfloat16),
            pltpu.VMEM((BUFS, BLK, BLK), jnp.float32),
            pltpu.SemaphoreType.DMA((BUFS,)),
        ],
        compiler_params=pltpu.CompilerParams(vmem_limit_bytes=32 * 2**20),
        cost_estimate=pl.CostEstimate(
            flops=32 * 3 * 2 * BLK * BLK * width, bytes_accessed=8 * 2**20, transcendentals=0
        ),
    )(count, place, source, target, *blocks, tiles)


def shift(value, axis, by):
    n = lax.axis_size(axis)
    return lax.ppermute(value, axis, [(i, (i + by) % n) for i in range(n)])


def ring_gather(value):
    n = lax.axis_size("bal")
    found = [value] + [None] * (n - 1)
    ahead = behind = value
    for hop in range(1, n // 2 + 1):
        ahead = shift(ahead, "bal", 1)
        found[hop] = ahead
        if n - hop > hop:
            behind = shift(behind, "bal", -1)
            found[n - hop] = behind
    return found


def spread(value, axes):
    return lax.all_to_all(value, axes, split_axis=0, concat_axis=0, tiled=True)


def summed_everywhere(term):
    rows, width = term.shape
    half = rows // 2
    core = lax.axis_index("core")
    mine = lax.dynamic_slice_in_dim(term, core * half, half, 0)
    other = lax.dynamic_slice_in_dim(term, (1 - core) * half, half, 0)
    mine = mine + shift(other, "core", 1)
    chips = ("y", "x", "bal")
    n = lax.axis_size(chips)
    row = spread(mine, chips).reshape(n, half // n, width).sum(0)
    back = jnp.broadcast_to(row[None], (n, half // n, width)).reshape(half, width)
    mine = spread(back, chips)
    other = shift(mine, "core", 1)
    first = jnp.where(core == 0, mine, other)
    second = jnp.where(core == 0, other, mine)
    return jnp.concatenate([first, second], axis=0)


def per_device(
    grad_out, deriv_mask, weight, zcache, tile_values, tile_source, tile_slot, recv_target
):
    rows, width = grad_out.shape
    n_bal = lax.axis_size("bal")
    chips = lax.axis_size(PLANE)
    bal = lax.axis_index("bal")
    core = lax.axis_index("core")

    tiles = lax.all_gather(tile_values, "bal", axis=0, tiled=True)
    wanted = spread(recv_target, GRP)
    code = (tile_slot // 2) * 64 + wanted[tile_slot] * 8 + tile_source
    per = code.shape[0]
    codes = spread(jnp.broadcast_to(code[None], (n_bal, per)).reshape(-1), "bal")
    group, block, source = codes // 64, (codes // 8) % 8, codes % 8
    chosen = block == bal
    n = codes.shape[0]
    order = jnp.arange(n, dtype=jnp.int32)
    rank = jnp.sum(jnp.where(chosen[None, :] & (order[None, :] < order[:, None]), 1, 0), axis=1)
    hit = (chosen & (order < n))[None, :] & (rank[None, :] == order[:, None])

    def pick(value):
        return jnp.sum(jnp.where(hit, value[None, :], 0), axis=1)

    count = jnp.sum(chosen.astype(jnp.int32)).reshape(1)
    place = pick(order)
    behind = pick((bal - source) % n_bal)
    target = pick(group // 2 + chips * ((group % 2) ^ core))

    mask_float = deriv_mask.astype(jnp.float32)
    fixed_grad = grad_out
    for step in range(STEPS):
        blocks = ring_gather(fixed_grad)
        keep, send = products(count, place, behind, target, blocks, tiles, chips)
        partial_sum = keep + shift(send, "core", 1)
        owned = spread(partial_sum, PLANE).reshape(chips, rows, width).sum(0)
        product = jnp.dot(owned, weight, precision=HIGHEST, preferred_element_type=jnp.float32)
        fixed_grad = mask_float * product + grad_out
    local_term = jnp.dot(
        fixed_grad.T, zcache, precision=HIGHEST, preferred_element_type=jnp.float32
    )
    return (summed_everywhere(local_term), fixed_grad)


def solution(mesh):
    fine = Mesh(mesh.devices.reshape(4, 4, 2, mesh.shape["bal"]), ALL)
    in_specs = (
        P(ALL, None),
        P(ALL, None),
        P(),
        P(ALL, None),
        P(ALL, None, None),
        P(ALL),
        P(ALL),
        P(ALL),
    )
    out_specs = (P(), P(ALL, None))
    return jax.shard_map(
        per_device, mesh=fine, in_specs=in_specs, out_specs=out_specs, check_vma=False
    )
```

time: 916 us -> 478 us (0.52)
  waiting for transfers between devices: 459 us -> 226 us
  blocking collectives: 326 us -> 114 us
  starting transfers between devices: 1.02 us -> 64.1 us
  matrix products: 52.9 us -> 1.26 us
  local copies, waits for them, and re-layouts: 55.4 us -> 21 us
  Pallas kernels: 0 us -> 33.6 us
    psum x1 -> x0, waiting for transfers between devices: 256 us -> none  [per_device(): weight_grad = lax.psum(local_term, ('grp', 'bal'))]
    all_to_all x3 -> x4, blocking collectives: 326 us -> 114 us  [spread(): return lax.all_to_all(value, axes, split_axis=0, concat_axis=0, tiled=True)]
    reduce_scatter x3 -> x0, waiting for transfers between devices: 89.7 us -> none  [per_device(): lax.psum_scatter(sums, 'bal', scatter_dimension=0, tiled=True)]
    ppermute x0 -> x26, waiting for transfers between devices: none -> 57.3 us  [shift(): return lax.ppermute(value, axis, [(i, (i + by) % n) for i in range(n)])]
    dot_general x10 -> x4, matrix products: 52.9 us -> 1.26 us  [the longest x3 0.85 us: per_device(): jnp.dot(owned, weight, precision=HIGHEST, preferred_element_type=jnp.floa...]
    ppermute x0 -> x26, starting transfers between devices: none -> 43.3 us  [shift(): return lax.ppermute(value, axis, [(i, (i + by) % n) for i in range(n)])]
    all_to_all x0 -> x3, waiting for transfers between devices: none -> 41 us  [spread(): return lax.all_to_all(value, axes, split_axis=0, concat_axis=0, tiled=True)]
    pallas_call x0 -> x3, Pallas kernels: none -> 33.6 us  [products(): pl.pallas_call(products_kernel, out_shape=(out, out), in_specs=[smem] * 4...]
  transfers between devices with their start and end apart: 7 -> 30, of which waited for: 7 -> 22; matrix products, arithmetic and copies ran while one was open for 0% -> 1% of each run, Pallas kernels for 0% -> 0%
where the time goes in v1:
time: 478 us; the launch traced here: 479 us
  waiting for transfers between devices  226 us (47%)
  blocking collectives  114 us (24%)
  starting transfers between devices  64.1 us (13%)
  Pallas kernels  33.6 us (7%)
  local copies, waits for them, and re-layouts  21 us (4%)
  between operations  14.3 us (3%)
  other arithmetic  5.87 us (1%)
    all_gather x1, waiting for transfers between devices, per_device(): tiles = lax.all_gather(tile_values, 'bal', axis=0, tiled=True)  126 us
    all_to_all x4, blocking collectives, spread(): return lax.all_to_all(value, axes, split_axis=0, concat_axis=0, tiled=True)  114 us
    ppermute x26, waiting for transfers between devices, shift(): return lax.ppermute(value, axis, [(i, (i + by) % n) for i in range(n)])  57.3 us
    ppermute x26, starting transfers between devices, shift(): return lax.ppermute(value, axis, [(i, (i + by) % n) for i in range(n)])  43.3 us
    all_to_all x3, waiting for transfers between devices, spread(): return lax.all_to_all(value, axes, split_axis=0, concat_axis=0, tiled=True)  41 us
    pallas_call x3, Pallas kernels, products(): pl.pallas_call(products_kernel, out_shape=(out, out), in_specs=[smem] * 4...  33.6 us
    all_to_all x3, starting transfers between devices, spread(): return lax.all_to_all(value, axes, split_axis=0, concat_axis=0, tiled=True)  20.8 us
    unnamed x23, local copies, waits for them, and re-layouts  18.1 us
  transfers between devices with their start and end apart: 30, of which 22 were waited for; matrix products, arithmetic and copies ran while one was open for 1% of the time, Pallas kernels for 0%

profile of v1, /device:TPU:1, one launch (start us, length us, event | category | flops | bytes accessed | tf_op | source)
XLA Modules:
  0.0 479.3 jit_solution(4449459629042256225)
XLA Ops:
  8.7 8.6 %all-to-all-start = ((s32[32,2,1]{1,2,0:T(1,128)}), s32[32,2,1]{1,2,0:T(1,128)S(1)}, u32[]{:S(2)}, u32[]{:S(2)}) async-start(s32[32,2,1]{1,2,0:T(1,128)} %bitcast), calls=%async_computation | async-start | bytes 32768 | tf_op jit(solution)/shard_map/all_to_all | solution.py:117
  19.0 5.1 %all-to-all-done = s32[32,2,1]{1,2,0:T(1,128)S(1)} async-done(((s32[32,2,1]{1,2,0:T(1,128)}), s32[32,2,1]{1,2,0:T(1,128)S(1)}, u32[]{:S(2)}, u32[]{:S(2)}) %all-to-all-start) | async-done | bytes 288 | tf_op jit(solution)/shard_map/all_to_all | solution.py:117
  26.8 8.2 %all-to-all-start.1 = ((s32[8,32,1]{1,2,0:T(1,128)}), s32[8,32,1]{1,2,0:T(1,128)S(1)}, u32[]{:S(2)}, u32[]{:S(2)}) async-start(s32[8,32,1]{1,2,0:T(1,128)} %all_to_all.49), calls=%async_computation.1 | async-start | bytes 8192 | tf_op jit(solution)/shard_map/all_to_all | solution.py:117
  46.7 5.0 %collective-permute-done.1.refs_2_ = f32[128,256]{1,0:T(8,128)S(1)} collective-permute-done((f32[128,256]{1,0:T(8,128)S(1)}, f32[128,256]{1,0:T(8,128)S(1)}, u32[]{:S(2)}, u32[]{:S(2)}) %collective-permute-start.1) | collective-permute-done | bytes 131104 | tf_op jit(solution)/shard_map/ppermute | solution.py:100
  55.5 4.7 collective-permute-done.2.refs_3_
  60.6 7.9 %collective-permute-done.3.refs_4_ = f32[128,256]{1,0:T(8,128)S(1)} collective-permute-done((f32[128,256]{1,0:T(8,128)S(1)}, f32[128,256]{1,0:T(8,128)S(1)}, u32[]{:S(2)}, u32[]{:S(2)}) %collective-permute-start.3) | collective-permute-done | bytes 131104 | tf_op jit(solution)/shard_map/ppermute | solution.py:100
  68.5 126.5 %all-gather.2.cloned.1.call-done.refs_8_ = f32[256,128,128]{2,1,0:T(8,128)} async-done(((f32[32,128,128]{2,1,0:T(8,128)}), f32[256,128,128]{2,1,0:T(8,128)}) %all-gather.2.cloned.1.call-update) | async-done | bytes 16777232 | tf_op jit(solution)/shard_map/all_gather | solution.py:147
  194.9 5.8 %copy-done.1 = f32[256,128,128]{2,1,0:T(8,128)S(1)} copy-done((f32[256,128,128]{2,1,0:T(8,128)S(1)}, f32[256,128,128]{2,1,0:T(8,128)}, u32[]{:S(2)}) %copy-start.1) | copy-done | bytes 16777240
  200.7 11.2 %shard_map.95 = (f32[2048,256]{1,0:T(8,128)S(1)}, f32[2048,256]{1,0:T(8,128)S(1)}) custom-call(s32[1]{0:T(128)} %bitcast.1.count, s32[256]{0:T(256)S(1)} %get-tuple-element.18.place, s32[256]{0:T(256)S(1)} %get-tuple-element.17.source, s32[256]{0:T(256)S(1)} %get-tuple-element.16.target, f32[128,256]{1,0:T(8,128)S(1)} %copy-done.4, ...), custom_call_target="tpu_custom_call" | custom-call | flops 805306368 | bytes 8388608 | tf_op jit(solution)/shard_map/pallas_call | solution.py:81
  212.0 4.1 collective-permute-done.7
  216.5 37.2 %all_to_all.69 = f32[16,128,256]{2,1,0:T(8,128)S(1)} all-to-all(f32[16,128,256]{2,1,0:T(8,128)S(1)} %bitcast.24), channel_id=1, replica_groups=mesh['y'=4,'x'=4,'core'=2,'bal'=8] {'y','x'}, dimensions={0} | all-to-all | bytes 4194304 | tf_op jit(solution)/shard_map/all_to_all | solution.py:117
  270.0 5.7 %collective-permute-done.11.refs_4_ = f32[128,256]{1,0:T(8,128)S(1)} collective-permute-done((f32[128,256]{1,0:T(8,128)S(1)}, f32[128,256]{1,0:T(8,128)S(1)}, u32[]{:S(2)}, u32[]{:S(2)}) %collective-permute-start.11) | collective-permute-done | bytes 131104 | tf_op jit(solution)/shard_map/ppermute | solution.py:100
  275.7 5.8 %copy-done.2 = f32[256,128,128]{2,1,0:T(8,128)S(1)} copy-done((f32[256,128,128]{2,1,0:T(8,128)S(1)}, f32[256,128,128]{2,1,0:T(8,128)}, u32[]{:S(2)}) %copy-start.2) | copy-done | bytes 16777240
  281.5 11.2 %shard_map.96 = (f32[2048,256]{1,0:T(8,128)S(1)}, f32[2048,256]{1,0:T(8,128)S(1)}) custom-call(s32[1]{0:T(128)} %bitcast.1.count, s32[256]{0:T(256)S(1)} %get-tuple-element.18.place, s32[256]{0:T(256)S(1)} %get-tuple-element.17.source, s32[256]{0:T(256)S(1)} %get-tuple-element.16.target, f32[128,256]{1,0:T(8,128)S(1)} %fusion.2.refs_0_, ...), custom_call_target="tpu_custom_call" | custom-call | flops 805306368 | bytes 8388608 | tf_op jit(solution)/shard_map/pallas_call | solution.py:81
  292.7 5.4 %collective-permute-start.15 = (f32[2048,256]{1,0:T(8,128)S(1)}, f32[2048,256]{1,0:T(8,128)S(1)}, u32[]{:S(2)}, u32[]{:S(2)}) collective-permute-start(f32[2048,256]{1,0:T(8,128)S(1)} %get-tuple-element.11), channel_id=1, source_target_pairs={{0,8},{8,0},{1,9},{9,1},{2,10},{10,2},{3,11},{11,3},{4,12},{12,4},... | collective-permute-start | bytes 6291464 | tf_op jit(solution)/shard_map/ppermute | solution.py:100
  302.2 31.4 %all_to_all.70 = f32[16,128,256]{2,1,0:T(8,128)S(1)} all-to-all(f32[16,128,256]{2,1,0:T(8,128)S(1)} %bitcast.25), channel_id=1, replica_groups=mesh['y'=4,'x'=4,'core'=2,'bal'=8] {'y','x'}, dimensions={0} | all-to-all | bytes 4194304 | tf_op jit(solution)/shard_map/all_to_all | solution.py:117
  349.7 5.5 %collective-permute-done.19.refs_4_ = f32[128,256]{1,0:T(8,128)S(1)} collective-permute-done((f32[128,256]{1,0:T(8,128)S(1)}, f32[128,256]{1,0:T(8,128)S(1)}, u32[]{:S(2)}, u32[]{:S(2)}) %collective-permute-start.19) | collective-permute-done | bytes 131104 | tf_op jit(solution)/shard_map/ppermute | solution.py:100
  355.1 5.8 %copy-done.3 = f32[256,128,128]{2,1,0:T(8,128)S(1)} copy-done((f32[256,128,128]{2,1,0:T(8,128)S(1)}, f32[256,128,128]{2,1,0:T(8,128)}, u32[]{:S(2)}) %copy-start.3) | copy-done | bytes 16777240
  360.9 11.2 %shard_map.97 = (f32[2048,256]{1,0:T(8,128)S(1)}, f32[2048,256]{1,0:T(8,128)S(1)}) custom-call(s32[1]{0:T(128)} %bitcast.1.count, s32[256]{0:T(256)S(1)} %get-tuple-element.18.place, s32[256]{0:T(256)S(1)} %get-tuple-element.17.source, s32[256]{0:T(256)S(1)} %get-tuple-element.16.target, f32[128,256]{1,0:T(8,128)S(1)} %fusion.1.refs_0_, ...), custom_call_target="tpu_custom_call" | custom-call | flops 805306368 | bytes 8388608 | tf_op jit(solution)/shard_map/pallas_call | solution.py:81
  372.1 5.6 %collective-permute-start.23 = (f32[2048,256]{1,0:T(8,128)S(1)}, f32[2048,256]{1,0:T(8,128)S(1)}, u32[]{:S(2)}, u32[]{:S(2)}) collective-permute-start(f32[2048,256]{1,0:T(8,128)S(1)} %get-tuple-element.13), channel_id=1, source_target_pairs={{0,8},{8,0},{1,9},{9,1},{2,10},{10,2},{3,11},{11,3},{4,12},{12,4},... | collective-permute-start | bytes 6291464 | tf_op jit(solution)/shard_map/ppermute | solution.py:100
  383.2 4.0 all-to-all-start.4
  387.2 32.0 %all-to-all-done.4 = f32[16,128,256]{2,1,0:T(8,128)S(1)} async-done(((f32[16,128,256]{2,1,0:T(8,128)}), f32[16,128,256]{2,1,0:T(8,128)S(1)}, u32[]{:S(2)}, u32[]{:S(2)}) %all-to-all-start.4) | async-done | bytes 2097184 | tf_op jit(solution)/shard_map/all_to_all | solution.py:117
  423.0 27.8 %all_to_all.71 = f32[128,1,256]{2,1,0:T(1,128)S(1)} all-to-all(f32[128,1,256]{2,1,0:T(1,128)S(1)} %copy.13), channel_id=1, replica_groups=mesh['y'=4,'x'=4,'core'=2,'bal'=8] {'y','x','bal'}, dimensions={0} | all-to-all | bytes 262144 | tf_op jit(solution)/shard_map/all_to_all | solution.py:117
  451.0 17.2 %all_to_all.72 = f32[128,1,256]{2,1,0:T(1,128)S(1)} all-to-all(f32[128,1,256]{2,1,0:T(1,128)S(1)} %reshape.179), channel_id=1, replica_groups=mesh['y'=4,'x'=4,'core'=2,'bal'=8] {'y','x','bal'}, dimensions={0} | all-to-all | bytes 262144 | tf_op jit(solution)/shard_map/all_to_all | solution.py:117
  (99 shorter events, 72.2 us)
Async XLA Ops:
  7.2 187.7 %all-gather.2.cloned.1.call-start = ((), (), s32[]{:S(2)}) async-start(), calls=%async_computation.7 | async-start | bytes 18874368 | tf_op jit(solution)/shard_map/all_gather | solution.py:147
  8.7 15.5 %all-to-all-start = ((s32[32,2,1]{1,2,0:T(1,128)}), s32[32,2,1]{1,2,0:T(1,128)S(1)}, u32[]{:S(2)}, u32[]{:S(2)}) async-start(s32[32,2,1]{1,2,0:T(1,128)} %bitcast), calls=%async_computation | async-start | bytes 32768 | tf_op jit(solution)/shard_map/all_to_all | solution.py:117
  17.3 25.6 %collective-permute-start = (f32[128,256]{1,0:T(8,128)S(1)}, f32[128,256]{1,0:T(8,128)S(1)}, u32[]{:S(2)}, u32[]{:S(2)}) collective-permute-start(f32[128,256]{1,0:T(8,128)S(1)} %copy-done.4), channel_id=1, source_target_pairs={{0,1},{1,2},{2,3},{3,4},{4,5},{5,6},{6,7},{7,0},{8,9},{9,10},{10,1... | collective-permute-start | bytes 393224 | tf_op jit(solution)/shard_map/ppermute | solution.py:100
  26.8 14.7 %all-to-all-start.1 = ((s32[8,32,1]{1,2,0:T(1,128)}), s32[8,32,1]{1,2,0:T(1,128)S(1)}, u32[]{:S(2)}, u32[]{:S(2)}) async-start(s32[8,32,1]{1,2,0:T(1,128)} %all_to_all.49), calls=%async_computation.1 | async-start | bytes 8192 | tf_op jit(solution)/shard_map/all_to_all | solution.py:117
  35.0 8.3 %collective-permute-start.4 = (f32[128,256]{1,0:T(8,128)S(1)}, f32[128,256]{1,0:T(8,128)S(1)}, u32[]{:S(2)}, u32[]{:S(2)}) collective-permute-start(f32[128,256]{1,0:T(8,128)S(1)} %copy-done.4), channel_id=1, source_target_pairs={{0,7},{1,0},{2,1},{3,2},{4,3},{5,4},{6,5},{7,6},{8,15},{9,8},{10,9... | collective-permute-start | bytes 393224 | tf_op jit(solution)/shard_map/ppermute | solution.py:100
  42.9 8.8 %collective-permute-start.1 = (f32[128,256]{1,0:T(8,128)S(1)}, f32[128,256]{1,0:T(8,128)S(1)}, u32[]{:S(2)}, u32[]{:S(2)}) collective-permute-start(f32[128,256]{1,0:T(8,128)S(1)} %collective-permute-done.refs_1_), channel_id=1, source_target_pairs={{0,1},{1,2},{2,3},{3,4},{4,5},{5,6},{6,7},{7,0},{8,9},{9,10},{10,1... | collective-permute-start | bytes 393224 | tf_op jit(solution)/shard_map/ppermute | solution.py:100
  43.3 8.8 %collective-permute-start.5 = (f32[128,256]{1,0:T(8,128)S(1)}, f32[128,256]{1,0:T(8,128)S(1)}, u32[]{:S(2)}, u32[]{:S(2)}) collective-permute-start(f32[128,256]{1,0:T(8,128)S(1)} %collective-permute-done.4.refs_7_), channel_id=1, source_target_pairs={{0,7},{1,0},{2,1},{3,2},{4,3},{5,4},{6,5},{7,6},{8,15},{9,8},{10,9... | collective-permute-start | bytes 393224 | tf_op jit(solution)/shard_map/ppermute | solution.py:100
  51.7 8.5 %collective-permute-start.2 = (f32[128,256]{1,0:T(8,128)S(1)}, f32[128,256]{1,0:T(8,128)S(1)}, u32[]{:S(2)}, u32[]{:S(2)}) collective-permute-start(f32[128,256]{1,0:T(8,128)S(1)} %collective-permute-done.1.refs_2_), channel_id=1, source_target_pairs={{0,1},{1,2},{2,3},{3,4},{4,5},{5,6},{6,7},{7,0},{8,9},{9,10},{10,1... | collective-permute-start | bytes 393224 | tf_op jit(solution)/shard_map/ppermute | solution.py:100
  52.0 8.6 %collective-permute-start.6 = (f32[128,256]{1,0:T(8,128)S(1)}, f32[128,256]{1,0:T(8,128)S(1)}, u32[]{:S(2)}, u32[]{:S(2)}) collective-permute-start(f32[128,256]{1,0:T(8,128)S(1)} %collective-permute-done.5.refs_6_), channel_id=1, source_target_pairs={{0,7},{1,0},{2,1},{3,2},{4,3},{5,4},{6,5},{7,6},{8,15},{9,8},{10,9... | collective-permute-start | bytes 393224 | tf_op jit(solution)/shard_map/ppermute | solution.py:100
  60.2 8.3 %collective-permute-start.3 = (f32[128,256]{1,0:T(8,128)S(1)}, f32[128,256]{1,0:T(8,128)S(1)}, u32[]{:S(2)}, u32[]{:S(2)}) collective-permute-start(f32[128,256]{1,0:T(8,128)S(1)} %collective-permute-done.2.refs_3_), channel_id=1, source_target_pairs={{0,1},{1,2},{2,3},{3,4},{4,5},{5,6},{6,7},{7,0},{8,9},{9,10},{10,1... | collective-permute-start | bytes 393224 | tf_op jit(solution)/shard_map/ppermute | solution.py:100
  254.8 5.1 %collective-permute-start.8 = (f32[128,256]{1,0:T(8,128)S(1)}, f32[128,256]{1,0:T(8,128)S(1)}, u32[]{:S(2)}, u32[]{:S(2)}) collective-permute-start(f32[128,256]{1,0:T(8,128)S(1)} %fusion.2.refs_0_), channel_id=1, source_target_pairs={{0,1},{1,2},{2,3},{3,4},{4,5},{5,6},{6,7},{7,0},{8,9},{9,10},{10,1... | collective-permute-start | bytes 393224 | tf_op jit(solution)/shard_map/ppermute | solution.py:100
  260.0 5.0 %collective-permute-start.9 = (f32[128,256]{1,0:T(8,128)S(1)}, f32[128,256]{1,0:T(8,128)S(1)}, u32[]{:S(2)}, u32[]{:S(2)}) collective-permute-start(f32[128,256]{1,0:T(8,128)S(1)} %collective-permute-done.8.refs_1_), channel_id=1, source_target_pairs={{0,1},{1,2},{2,3},{3,4},{4,5},{5,6},{6,7},{7,0},{8,9},{9,10},{10,1... | collective-permute-start | bytes 393224 | tf_op jit(solution)/shard_map/ppermute | solution.py:100
  260.0 5.0 %collective-permute-start.13 = (f32[128,256]{1,0:T(8,128)S(1)}, f32[128,256]{1,0:T(8,128)S(1)}, u32[]{:S(2)}, u32[]{:S(2)}) collective-permute-start(f32[128,256]{1,0:T(8,128)S(1)} %collective-permute-done.12.refs_7_), channel_id=1, source_target_pairs={{0,7},{1,0},{2,1},{3,2},{4,3},{5,4},{6,5},{7,6},{8,15},{9,8},{10,9... | collective-permute-start | bytes 393224 | tf_op jit(solution)/shard_map/ppermute | solution.py:100
  265.0 5.0 %collective-permute-start.10 = (f32[128,256]{1,0:T(8,128)S(1)}, f32[128,256]{1,0:T(8,128)S(1)}, u32[]{:S(2)}, u32[]{:S(2)}) collective-permute-start(f32[128,256]{1,0:T(8,128)S(1)} %collective-permute-done.9.refs_2_), channel_id=1, source_target_pairs={{0,1},{1,2},{2,3},{3,4},{4,5},{5,6},{6,7},{7,0},{8,9},{9,10},{10,1... | collective-permute-start | bytes 393224 | tf_op jit(solution)/shard_map/ppermute | solution.py:100
  265.0 5.0 %collective-permute-start.14 = (f32[128,256]{1,0:T(8,128)S(1)}, f32[128,256]{1,0:T(8,128)S(1)}, u32[]{:S(2)}, u32[]{:S(2)}) collective-permute-start(f32[128,256]{1,0:T(8,128)S(1)} %collective-permute-done.13.refs_6_), channel_id=1, source_target_pairs={{0,7},{1,0},{2,1},{3,2},{4,3},{5,4},{6,5},{7,6},{8,15},{9,8},{10,9... | collective-permute-start | bytes 393224 | tf_op jit(solution)/shard_map/ppermute | solution.py:100
  270.0 5.7 %collective-permute-start.11 = (f32[128,256]{1,0:T(8,128)S(1)}, f32[128,256]{1,0:T(8,128)S(1)}, u32[]{:S(2)}, u32[]{:S(2)}) collective-permute-start(f32[128,256]{1,0:T(8,128)S(1)} %collective-permute-done.10.refs_3_), channel_id=1, source_target_pairs={{0,1},{1,2},{2,3},{3,4},{4,5},{5,6},{6,7},{7,0},{8,9},{9,10},{10,1... | collective-permute-start | bytes 393224 | tf_op jit(solution)/shard_map/ppermute | solution.py:100
  292.7 9.2 %collective-permute-start.15 = (f32[2048,256]{1,0:T(8,128)S(1)}, f32[2048,256]{1,0:T(8,128)S(1)}, u32[]{:S(2)}, u32[]{:S(2)}) collective-permute-start(f32[2048,256]{1,0:T(8,128)S(1)} %get-tuple-element.11), channel_id=1, source_target_pairs={{0,8},{8,0},{1,9},{9,1},{2,10},{10,2},{3,11},{11,3},{4,12},{12,4},... | collective-permute-start | bytes 6291464 | tf_op jit(solution)/shard_map/ppermute | solution.py:100
  334.0 5.1 %collective-permute-start.16 = (f32[128,256]{1,0:T(8,128)S(1)}, f32[128,256]{1,0:T(8,128)S(1)}, u32[]{:S(2)}, u32[]{:S(2)}) collective-permute-start(f32[128,256]{1,0:T(8,128)S(1)} %fusion.1.refs_0_), channel_id=1, source_target_pairs={{0,1},{1,2},{2,3},{3,4},{4,5},{5,6},{6,7},{7,0},{8,9},{9,10},{10,1... | collective-permute-start | bytes 393224 | tf_op jit(solution)/shard_map/ppermute | solution.py:100
  339.1 5.0 %collective-permute-start.17 = (f32[128,256]{1,0:T(8,128)S(1)}, f32[128,256]{1,0:T(8,128)S(1)}, u32[]{:S(2)}, u32[]{:S(2)}) collective-permute-start(f32[128,256]{1,0:T(8,128)S(1)} %collective-permute-done.16.refs_1_), channel_id=1, source_target_pairs={{0,1},{1,2},{2,3},{3,4},{4,5},{5,6},{6,7},{7,0},{8,9},{9,10},{10,1... | collective-permute-start | bytes 393224 | tf_op jit(solution)/shard_map/ppermute | solution.py:100
  339.2 5.0 %collective-permute-start.21 = (f32[128,256]{1,0:T(8,128)S(1)}, f32[128,256]{1,0:T(8,128)S(1)}, u32[]{:S(2)}, u32[]{:S(2)}) collective-permute-start(f32[128,256]{1,0:T(8,128)S(1)} %collective-permute-done.20.refs_7_), channel_id=1, source_target_pairs={{0,7},{1,0},{2,1},{3,2},{4,3},{5,4},{6,5},{7,6},{8,15},{9,8},{10,9... | collective-permute-start | bytes 393224 | tf_op jit(solution)/shard_map/ppermute | solution.py:100
  344.2 5.5 %collective-permute-start.22 = (f32[128,256]{1,0:T(8,128)S(1)}, f32[128,256]{1,0:T(8,128)S(1)}, u32[]{:S(2)}, u32[]{:S(2)}) collective-permute-start(f32[128,256]{1,0:T(8,128)S(1)} %collective-permute-done.21.refs_6_), channel_id=1, source_target_pairs={{0,7},{1,0},{2,1},{3,2},{4,3},{5,4},{6,5},{7,6},{8,15},{9,8},{10,9... | collective-permute-start | bytes 393224 | tf_op jit(solution)/shard_map/ppermute | solution.py:100
  349.2 5.9 %collective-permute-start.19 = (f32[128,256]{1,0:T(8,128)S(1)}, f32[128,256]{1,0:T(8,128)S(1)}, u32[]{:S(2)}, u32[]{:S(2)}) collective-permute-start(f32[128,256]{1,0:T(8,128)S(1)} %collective-permute-done.18.refs_3_), channel_id=1, source_target_pairs={{0,1},{1,2},{2,3},{3,4},{4,5},{5,6},{6,7},{7,0},{8,9},{9,10},{10,1... | collective-permute-start | bytes 393224 | tf_op jit(solution)/shard_map/ppermute | solution.py:100
  372.1 9.4 %collective-permute-start.23 = (f32[2048,256]{1,0:T(8,128)S(1)}, f32[2048,256]{1,0:T(8,128)S(1)}, u32[]{:S(2)}, u32[]{:S(2)}) collective-permute-start(f32[2048,256]{1,0:T(8,128)S(1)} %get-tuple-element.13), channel_id=1, source_target_pairs={{0,8},{8,0},{1,9},{9,1},{2,10},{10,2},{3,11},{11,3},{4,12},{12,4},... | collective-permute-start | bytes 6291464 | tf_op jit(solution)/shard_map/ppermute | solution.py:100
  383.2 36.0 %all-to-all-start.4 = ((f32[16,128,256]{2,1,0:T(8,128)}), f32[16,128,256]{2,1,0:T(8,128)S(1)}, u32[]{:S(2)}, u32[]{:S(2)}) async-start(f32[16,128,256]{2,1,0:T(8,128)} %bitcast.4), calls=%async_computation.4 | async-start | bytes 4194304 | tf_op jit(solution)/shard_map/all_to_all | solution.py:117
  (17 other events, 417.2 us)
Sparse Core Ops, SparseCore 0:
  9.8 185.0 all-gather.1
